TPU v7x, 256 devices: a whole 4x4x8 slice. The times are simulated.
256 devices in a mesh: row: 4 (over y), col: 16 (over x, z_lo, core), depth: 4 (over z_hi).
Axes of the slice: x: 4, y: 4, z: 8 (z_hi: 4, z_lo: 2; z = z_hi * 2 + z_lo), core: 2. Of those that a mesh axis runs over, the one named last changes fastest.
Arguments:
- left_pair: bfloat16 [512, 4, 512, 128], P('row', 'depth', 'col'), may hold values from -6 to 6
- right_pair: bfloat16 [832, 4, 512, 128], P('col', 'depth', 'row'), may hold values from -6 to 6
- pair_tile: bfloat16 [512, 832, 128], P('row', ('col', 'depth')), may hold values from -6 to 6
- row_flags: int32 [512], P('row'), may hold values 0 or 1
- column_flags: int32 [832], P('col'), may hold values 0 or 1
- key_flags: int32 [4, 512], replicated, may hold values 0 or 1
- input_gain: float32 [128], replicated, may hold values from 0.5 to 1.5
- input_bias: float32 [128], replicated, may hold values from -1.75 to 1.75
- left_gate_weight: bfloat16 [128, 128], replicated, may hold values from -0.5 to 0.5
- left_value_weight: bfloat16 [128, 128], replicated, may hold values from -0.5 to 0.5
- right_gate_weight: bfloat16 [128, 128], replicated, may hold values from -0.5 to 0.5
- right_value_weight: bfloat16 [128, 128], replicated, may hold values from -0.5 to 0.5
- hidden_gain: float32 [128], replicated, may hold values from 0.5 to 1.5
- hidden_bias: float32 [128], replicated, may hold values from -1.75 to 1.75
- output_gate_weight: bfloat16 [128, 128], replicated, may hold values from -0.5 to 0.5
- output_weight: bfloat16 [128, 128], replicated, may hold values from -0.5 to 0.5
Outputs:
- update: bfloat16 [512, 832, 128], P('row', ('col', 'depth'))
All inputs are finite; a program needn't handle non-finite values. No bound on the sum of `row_flags` or of `column_flags` on one device may be relied on, other than what follows from the above.
Results may differ from a plain program's by a relative error of at most 0.0055.
Values may be sent and summed in bfloat16 or wider, within the bound.
A program may use at most 128 MiB of HBM per device.

v0:
```python
import jax
import jax.numpy as jnp
from jax import lax
from jax.sharding import PartitionSpec as P

EPSILON = 1e-05


def layer_norm(values, norm_gain, norm_bias):
    widened = values.astype(jnp.float32)
    centre = jnp.mean(widened, axis=-1, keepdims=True)
    shifted = widened - centre
    spread = jnp.mean(shifted * shifted, axis=-1, keepdims=True)
    scaled = shifted * lax.rsqrt(spread + EPSILON) * norm_gain + norm_bias
    return scaled.astype(jnp.bfloat16)


def gated_values(pair, input_gain, input_bias, gate_weight, value_weight, mask):
    normed = layer_norm(pair, input_gain, input_bias)
    gating = jax.nn.sigmoid(jnp.dot(normed, gate_weight, preferred_element_type=jnp.float32))
    content = jnp.dot(normed, value_weight, preferred_element_type=jnp.float32)
    return (mask[..., None] * gating * content).astype(jnp.bfloat16)


def per_device(
    left_pair,
    right_pair,
    pair_tile,
    row_flags,
    column_flags,
    key_flags,
    input_gain,
    input_bias,
    left_gate_weight,
    left_value_weight,
    right_gate_weight,
    right_value_weight,
    hidden_gain,
    hidden_bias,
    output_gate_weight,
    output_weight,
):
    depth_index = lax.axis_index("depth")
    column_index = lax.axis_index("col")
    row_index = lax.axis_index("row")
    left_width = left_pair.shape[2]
    right_width = right_pair.shape[2]
    left_keys = lax.dynamic_slice(
        key_flags, (depth_index, column_index * left_width), (1, left_width)
    ).astype(jnp.float32)
    right_keys = lax.dynamic_slice(
        key_flags, (depth_index, row_index * right_width), (1, right_width)
    ).astype(jnp.float32)
    left_mask = row_flags.astype(jnp.float32)[:, None, None] * left_keys[None, :, :]
    right_mask = column_flags.astype(jnp.float32)[:, None, None] * right_keys[None, :, :]
    left_act = gated_values(
        left_pair, input_gain, input_bias, left_gate_weight, left_value_weight, left_mask
    )
    right_act = gated_values(
        right_pair, input_gain, input_bias, right_gate_weight, right_value_weight, right_mask
    )
    right_full = lax.all_gather(right_act, "row", axis=2, tiled=True)
    combined = jnp.einsum(
        "iqmh,jqmh->ijh",
        lax.all_gather(left_act, "col", axis=2, tiled=True),
        right_full,
        preferred_element_type=jnp.float32,
    )
    owned = lax.psum_scatter(combined, "depth", scatter_dimension=1, tiled=True)
    hidden_normed = layer_norm(owned, hidden_gain, hidden_bias)
    tile_normed = layer_norm(pair_tile, input_gain, input_bias)
    gating = jax.nn.sigmoid(
        jnp.dot(tile_normed, output_gate_weight, preferred_element_type=jnp.float32)
    )
    projected = jnp.dot(hidden_normed, output_weight, preferred_element_type=jnp.float32)
    return (gating * projected).astype(jnp.bfloat16)


def solution(mesh):
    in_specs = (
        P("row", "depth", "col", None),
        P("col", "depth", "row", None),
        P("row", ("col", "depth"), None),
        P("row"),
        P("col"),
        P(),
        P(),
        P(),
        P(),
        P(),
        P(),
        P(),
        P(),
        P(),
        P(),
        P(),
    )
    out_specs = P("row", ("col", "depth"), None)
    return jax.shard_map(
        per_device, mesh=mesh, in_specs=in_specs, out_specs=out_specs, check_vma=False
    )
```

profile of v0, /device:TPU:1, one launch (start us, length us, event | category | flops | bytes accessed | tf_op | source)
XLA Modules:
  0.0 317.6 jit_solution(8346426470531011996)
XLA Ops:
  6.6 0.8 convert_element_type.50
  7.4 2.0 convert_reduce_fusion
  9.4 2.1 fusion.2
  11.5 3.8 %fusion.22 = f32[52,128,128]{2,1,0:T(8,128)} fusion(bf16[52,1,128,128]{3,2,1,0:T(8,128)(2,1)S(1)} %copy-done.1, f32[128]{0:T(128)S(1)} %copy-done.9, f32[128]{0:T(128)S(1)} %copy-done.10, f32[52,128]{1,0:T(8,128)S(1)} %add_rsqrt_fusion.1, f32[52,128]{1,0:T(8,128)S(1)} %broadcast_multiply_fusion.1, bf16[128,128]{1,0:T(8,128)(2,1)S(1)} %copy-done), kind=kOutput, calls=%fused_computation.32 | convolution fusion | flops 223215616 | bytes 5198848 | tf_op jit(solution)/shard_map/dot_general | solution.py:20
  15.4 4.4 %copy.19 = f32[52,128,128]{1,0,2:T(8,128)} copy(f32[52,128,128]{2,1,0:T(8,128)} %fusion.22) | data formatting | bytes 6815744 | tf_op jit(solution)/shard_map/dot_general | solution.py:20
  19.8 3.9 %fusion.20 = f32[52,128,128]{2,1,0:T(8,128)} fusion(bf16[52,1,128,128]{3,2,1,0:T(8,128)(2,1)S(1)} %copy-done.1, f32[128]{0:T(128)S(1)} %copy-done.9, f32[128]{0:T(128)S(1)} %copy-done.10, f32[52,128]{1,0:T(8,128)S(1)} %add_rsqrt_fusion.1, f32[52,128]{1,0:T(8,128)S(1)} %broadcast_multiply_fusion.1, bf16[128,128]{1,0:T(8,128)(2,1)S(1)} %copy-done.5), kind=kOutput, calls=%fused_computation.31 | convolution fusion | flops 223215616 | bytes 5198848 | tf_op jit(solution)/shard_map/dot_general | solution.py:21
  23.6 4.4 %copy.20 = f32[52,128,128]{1,0,2:T(8,128)} copy(f32[52,128,128]{2,1,0:T(8,128)} %fusion.20) | data formatting | bytes 6815744 | tf_op jit(solution)/shard_map/dot_general | solution.py:21
  28.0 0.8 convert_bitcast_fusion.1
  28.8 0.1 broadcast_multiply_fusion.2
  28.8 5.5 %multiply_convert_fusion = bf16[52,128,128]{1,0,2:T(8,128)(2,1)} fusion(f32[52,128,128]{1,0,2:T(8,128)} %copy.20, f32[52,128,128]{1,0,2:T(8,128)} %copy.19, f32[52,128]{1,0:T(8,128)S(1)} %broadcast_multiply_fusion.2), kind=kLoop, calls=%fused_computation.4 | loop fusion | flops 5111808 | bytes 8546304 | tf_op jit(solution)/shard_map/convert_element_type | solution.py:22
  34.4 1.1 copy-done.2
  35.5 0.6 convert_reduce_fusion.1
  36.2 1.3 fusion.8
  37.5 1.3 fusion.30
  38.7 2.3 copy.21
  41.1 1.3 fusion.28
  42.3 2.3 copy.22
  44.7 0.8 convert_bitcast_fusion
  45.5 3.7 %multiply_convert_fusion.1 = bf16[128,32,128]{0,1,2:T(8,128)(2,1)} fusion(f32[128,32,128]{0,1,2:T(8,128)} %copy.22, f32[128,32,128]{0,1,2:T(8,128)} %copy.21, f32[128,32]{0,1:T(8,128)S(1)} %broadcast_multiply_fusion.3), kind=kLoop, calls=%fused_computation.17 | loop fusion | flops 3145728 | bytes 5259264 | tf_op jit(solution)/shard_map/convert_element_type | solution.py:22
  49.3 0.2 reduce-scatter.2.cloned.1.call-start
  49.5 68.8 %all-gather.5.cloned.1.call-done = bf16[52,512,128]{1,0,2:T(8,128)(2,1)} async-done(((bf16[52,128,128]{1,0,2:T(8,128)(2,1)}), bf16[52,512,128]{1,0,2:T(8,128)(2,1)}) %all-gather.5.cloned.1.call-update) | async-done | bytes 6815760 | tf_op jit(solution)/shard_map/all_gather | solution.py:62
  118.3 98.1 %all-gather.7.cloned.1.call-done = bf16[128,512,128]{0,1,2:T(8,128)(2,1)} async-done(((bf16[128,32,128]{0,1,2:T(8,128)(2,1)}), bf16[128,512,128]{0,1,2:T(8,128)(2,1)}) %all-gather.7.cloned.1.call-update) | async-done | bytes 16777232 | tf_op jit(solution)/shard_map/all_gather | solution.py:65
  216.4 13.0 %convolution_bitcast_fusion = f32[128,52,128]{0,1,2:T(8,128)} fusion(bf16[52,512,128]{1,0,2:T(8,128)(2,1)} %all-gather.5.cloned.1.call-done, bf16[128,512,128]{0,1,2:T(8,128)(2,1)} %all-gather.7.cloned.1.call-done), kind=kOutput, calls=%fused_computation.18 | convolution fusion | flops 872415232 | bytes 27000832 | tf_op jit(solution)/shard_map/iqmh,jqmh->ijh/dot_general | solution.py:63
  229.4 4.6 %copy.18 = f32[128,52,128]{2,0,1:T(8,128)} copy(f32[128,52,128]{0,1,2:T(8,128)} %convolution_bitcast_fusion) | data formatting | bytes 6815744 | tf_op jit(solution)/shard_map/iqmh,jqmh->ijh/transpose | solution.py:63
  234.0 1.0 copy-done.4
  235.0 0.2 convert_reduce_fusion.2
  235.2 0.6 fusion.24
  235.8 0.6 fusion.15
  236.5 69.9 %reduce-scatter.2.cloned.1.call-done = f32[128,13,128]{2,0,1:T(8,128)} async-done(((f32[128,52,128]{2,0,1:T(8,128)}), f32[128,13,128]{2,0,1:T(8,128)}) %reduce-scatter.2.cloned.1.call-update) | async-done | bytes 851984 | tf_op jit(solution)/shard_map/reduce_scatter | solution.py:69
  306.4 1.5 reduce_sum.78
  307.9 1.7 multiply_reduce_fusion
  309.7 1.4 fusion.16
  (43 shorter events, 0.3 us)
Async XLA Ops:
  6.5 5.0 %copy-start = (bf16[128,128]{1,0:T(8,128)(2,1)S(1)}, bf16[128,128]{1,0:T(8,128)(2,1)}, u32[]{:S(2)}) copy-start(bf16[128,128]{1,0:T(8,128)(2,1)} %param.26) | copy-start | bytes 98308
  6.5 2.8 copy-start.1
  6.5 5.0 %copy-start.10 = (f32[128]{0:T(128)S(1)}, f32[128]{0:T(128)}, u32[]{:S(2)}) copy-start(f32[128]{0:T(128)} %param.22) | copy-start | bytes 1540
  6.5 5.0 %copy-start.9 = (f32[128]{0:T(128)S(1)}, f32[128]{0:T(128)}, u32[]{:S(2)}) copy-start(f32[128]{0:T(128)} %param.23) | copy-start | bytes 1540
  6.5 111.8 %all-gather.5.cloned.1.call-start = ((), (), s32[]{:S(2)}) async-start(), calls=%async_computation.2 | async-start | bytes 9175040 | tf_op jit(solution)/shard_map/all_gather | solution.py:62
  15.4 4.4 %copy-start.5 = (bf16[128,128]{1,0:T(8,128)(2,1)S(1)}, bf16[128,128]{1,0:T(8,128)(2,1)}, u32[]{:S(2)}) copy-start(bf16[128,128]{1,0:T(8,128)(2,1)} %param.27) | copy-start | bytes 98308
  28.8 5.5 %copy-start.14 = (s32[128]{0:T(128)S(1)}, s32[128]{0:T(128)}, u32[]{:S(2)}) copy-start(s32[128]{0:T(128)} %param.19) | copy-start | bytes 1540
  34.3 1.2 copy-start.2
  34.3 3.2 copy-start.6
  34.3 182.1 %all-gather.7.cloned.1.call-start = ((), (), s32[]{:S(2)}) async-start(), calls=%async_computation.3 | async-start | bytes 17825792 | tf_op jit(solution)/shard_map/all_gather | solution.py:65
  38.7 2.3 copy-start.7
  49.3 257.1 %reduce-scatter.2.cloned.1.call-start = ((), (), s32[]{:S(2)}) async-start(), calls=%async_computation.1 | async-start | bytes 4259840 | tf_op jit(solution)/shard_map/reduce_scatter | solution.py:69
  234.0 1.0 copy-start.4
  234.0 1.8 copy-start.13
  235.8 73.8 %copy-start.8 = (bf16[128,128]{1,0:T(8,128)(2,1)S(1)}, bf16[128,128]{1,0:T(8,128)(2,1)}, u32[]{:S(2)}) copy-start(bf16[128,128]{1,0:T(8,128)(2,1)} %param.31) | copy-start | bytes 98308
  235.8 73.8 %copy-start.11 = (f32[128]{0:T(128)S(1)}, f32[128]{0:T(128)}, u32[]{:S(2)}) copy-start(f32[128]{0:T(128)} %param.29) | copy-start | bytes 1540
  235.8 73.8 %copy-start.12 = (f32[128]{0:T(128)S(1)}, f32[128]{0:T(128)}, u32[]{:S(2)}) copy-start(f32[128]{0:T(128)} %param.28) | copy-start | bytes 1540
  306.4 3.3 %copy-start.3 = (f32[128,13,128]{2,0,1:T(8,128)S(1)}, f32[128,13,128]{2,0,1:T(8,128)}, u32[]{:S(2)}) copy-start(f32[128,13,128]{2,0,1:T(8,128)} %reduce-scatter.2.cloned.1.call-done) | copy-start | bytes 2555908
Sparse Core Ops, SparseCore 0:
  34.4 83.8 all-gather.4
  120.1 96.2 all-gather.6
  234.1 72.1 reduce-scatter.1
where the time goes:
time: 318 us
  waiting for transfers between devices  237 us (75%)
  matrix products  25.3 us (8%)
  other arithmetic  21.7 us (7%)
  local copies, waits for them, and re-layouts  20.2 us (6%)
  between operations  13.3 us (4%)
    all_gather x1, waiting for transfers between devices, per_device(): lax.all_gather(left_act, 'col', axis=2, tiled=True)  98.1 us
    reduce_scatter x1, waiting for transfers between devices, per_device(): owned = lax.psum_scatter(combined, 'depth', scatter_dimension=1, tiled=True)  69.9 us
    all_gather x1, waiting for transfers between devices, per_device(): right_full = lax.all_gather(right_act, 'row', axis=2, tiled=True)  68.8 us
    dot_general x1, matrix products, per_device(): jnp.einsum('iqmh,jqmh->ijh', lax.all_gather(left_act, 'col', axis=2, tile...  13 us
    convert_element_type x2, other arithmetic, gated_values(): return (mask[..., None] * gating * content).astype(jnp.bfloat16)  9.2 us
    dot_general x2, local copies, waits for them, and re-layouts, gated_values(): content = jnp.dot(normed, value_weight, preferred_element_type=jnp.float32)  6.72 us
    dot_general x2, local copies, waits for them, and re-layouts, gated_values(): jnp.dot(normed, gate_weight, preferred_element_type=jnp.float32)  6.71 us
  transfers between devices with their start and end apart: 3, of which 3 were waited for; matrix products, arithmetic and copies ran while one was open for 5% of the time, Pallas kernels for 0%

commit v1 on v0

v1 whole, which is shorter than its diff:
```python
import functools

import jax
import jax.numpy as jnp
from jax import lax
from jax.experimental import pallas as pl
from jax.experimental.pallas import tpu as pltpu
from jax.sharding import PartitionSpec as P

EPSILON = 1e-05
MESH = pl.DeviceIdType.MESH
F32 = jnp.float32
BF16 = jnp.bfloat16

NI, NM, NJ, NK, NT = 128, 32, 52, 128, 13
HB = 8
JPAD = NT + 1
MSG = JPAD * HB
SLOTS = 80
BASE = 16

ROUND = (2, 1, 3, 0)
NEAR = [(dx, dy) for dx in ROUND for dy in ROUND]


def normalise(values):
    centre = jnp.mean(values, axis=-1, keepdims=True)
    shifted = values - centre
    spread = jnp.mean(shifted * shifted, axis=-1, keepdims=True)
    return shifted * lax.rsqrt(spread + EPSILON)


def sigmoid(values):
    return 0.5 * jnp.tanh(0.5 * values) + 0.5


def dot_nt(left, right):
    return lax.dot_general(left, right, (((1,), (1,)), ((), ())), preferred_element_type=F32)


def kernel(
    xl, xr, xt, row_flags, column_flags, key_scalars, key_rows,
    gain, bias, wlg, wlv, wrg, wrv, hgain, hbias, wog, wo,
    out,
    nl, tl, tr, ls, lb, rs, rb, osc, os_, cb, gate, fin,
    sl, rl, sr, rr, sf, rf, so, ro, cs,
):
    row = lax.axis_index("row")
    col = lax.axis_index("col")
    depth = lax.axis_index("depth")
    x = lax.div(col, 4)
    low = lax.rem(col, 4)
    core_mate = x * 4 + low + 1 - 2 * lax.rem(low, 2)
    mate_low = lax.rem(low + 2, 4)
    z_mate = x * 4 + mate_low
    other_low = low + 1 - 2 * lax.rem(low, 2)

    def at(dx, dy, dz=0):
        return (
            lax.rem(row + dy, 4),
            lax.rem(x + dx, 4) * 4 + low,
            lax.rem(depth + dz, 4),
        )

    barrier = pltpu.get_barrier_semaphore()
    peers = [at(dx, dy, dz) for dz in range(4) for dx, dy in NEAR if (dx, dy, dz) != (0, 0, 0)]
    peers += [(row, core_mate, depth), (row, z_mate, depth)]
    for peer in peers:
        pl.semaphore_signal(barrier, inc=1, device_id=peer, device_id_type=MESH)

    gains, biases = gain[...], bias[...]

    def left_norm(step, carry):
        rows = pl.ds(pl.multiple_of(step * 256, 256), 256)
        nl[rows, :] = normalise(xl[rows, :].astype(F32)) * gains + biases
        return carry

    lax.fori_loop(0, NI * NM // 256, left_norm, 0)
    w_left = jnp.concatenate([wlg[...], wlv[...]], axis=1).astype(F32).T.astype(BF16)
    row_mask = row_flags[...].astype(F32)

    def left_act(step, carry):
        xs = jnp.concatenate(
            [nl[pl.ds(step * 4 + mm, NI, stride=NM), :] for mm in range(4)], axis=0
        ).astype(BF16)
        both = dot_nt(w_left, xs)
        act = sigmoid(both[:128]) * both[128:]
        for mm in range(4):
            key = key_scalars[depth, col * NM + step * 4 + mm].astype(F32)
            part = act[:, mm * NI : (mm + 1) * NI] * (row_mask * key)
            for d in range(16):
                tl[pl.ds(d * HB * NM + step * 4 + mm, HB, stride=NM), :] = part[d * HB : (d + 1) * HB]
        return carry

    lax.fori_loop(0, NM // 4, left_act, 0)

    pl.semaphore_wait(barrier, len(peers))

    def owner(dx, dy):
        return lax.rem(x + dx, 4) * 4 + lax.rem(row + dy, 4)

    left_sends = {}
    for n, (dx, dy) in enumerate(NEAR):
        d = owner(dx, dy)
        rows = pl.ds(pl.multiple_of(d * HB * NM, HB * NM), HB * NM)
        ls[d] = tl[rows, :].astype(BF16).reshape(HB, NM, NI)
        target = lb.at[row, :, x, low]
        if (dx, dy) == (0, 0):
            pltpu.make_async_copy(ls.at[d], target, cs.at[0]).start()
            continue
        copy = pltpu.make_async_remote_copy(
            src_ref=ls.at[d], dst_ref=target, send_sem=sl.at[n], recv_sem=rl.at[n],
            device_id=at(dx, dy), device_id_type=MESH,
        )
        copy.start()
        left_sends[dx, dy] = copy

    w_right = jnp.concatenate([wrg[...], wrv[...]], axis=1).astype(F32).T.astype(BF16)
    key_block = key_rows[:, pl.ds(pl.multiple_of(row * NK, NK), NK)].astype(F32)
    here = lax.broadcasted_iota(jnp.int32, (4, NK), 0) == depth
    key_mask = jnp.sum(jnp.where(here, key_block, 0.0), axis=0, keepdims=True)

    def right_act(step, carry):
        rows = pl.ds(pl.multiple_of(step * 512, 512), 512)
        xs = (normalise(xr[rows, :].astype(F32)) * gains + biases).astype(BF16)
        both = dot_nt(w_right, xs)
        act = sigmoid(both[:128]) * both[128:]
        for jj in range(4):
            flag = column_flags[step * 4 + jj].astype(F32)
            part = act[:, jj * NK : (jj + 1) * NK] * (key_mask * flag)
            for d in range(16):
                tr[pl.ds(d * HB * NJ + step * 4 + jj, HB, stride=NJ), :] = part[d * HB : (d + 1) * HB]
        return carry

    lax.fori_loop(0, NJ // 4, right_act, 0)

    right_sends = {}
    for n, (dx, dy) in enumerate(NEAR):
        d = owner(dx, dy)
        rows = pl.ds(pl.multiple_of(d * HB * NJ, HB * NJ), HB * NJ)
        if (dx, dy) == (0, 0):
            rb[x, row] = tr[rows, :].astype(BF16)
            continue
        rs[d] = tr[rows, :].astype(BF16)
        copy = pltpu.make_async_remote_copy(
            src_ref=rs.at[d], dst_ref=rb.at[x, row], send_sem=sr.at[n], recv_sem=rr.at[n],
            device_id=at(dx, dy), device_id_type=MESH,
        )
        copy.start()
        right_sends[dx, dy] = copy

    def received(n, dst, sem):
        pltpu.make_async_remote_copy(
            src_ref=dst, dst_ref=dst, send_sem=sem, recv_sem=sem,
            device_id=at(1, 0), device_id_type=MESH,
        ).wait_recv()

    def source(dx, dy):
        return lax.rem(x + 4 - dx, 4), lax.rem(row + 4 - dy, 4)

    forwards = []

    def forward(n, y_from, share, device):
        part = lb.at[y_from, :, :, share]
        copy = pltpu.make_async_remote_copy(
            src_ref=part, dst_ref=part, send_sem=sf.at[n], recv_sem=rf.at[n],
            device_id=device, device_id_type=MESH,
        )
        copy.start()
        forwards.append(copy)

    pltpu.make_async_copy(ls.at[owner(0, 0)], lb.at[row, :, x, low], cs.at[0]).wait()
    for g, dy in enumerate(ROUND):
        for dx in ROUND:
            if (dx, dy) != (0, 0):
                x_from, y_from = source(dx, dy)
                n = NEAR.index((dx, dy))
                received(n, lb.at[y_from, :, x_from, low], rl.at[n])
        y_from = lax.rem(row + 4 - dy, 4)
        forward(g, y_from, low, (row, z_mate, depth))
        forward(4 + g, y_from, low, (row, core_mate, depth))

    tile_weight = wog[...]

    def tile_gate(step, carry):
        rows = pl.ds(step * 16, 16)
        padded = jnp.concatenate(
            [xt[rows].astype(F32), jnp.zeros((16, 16 - NT, 128), F32)], axis=1
        ).reshape(256, 128)
        normed = (normalise(padded) * gains + biases).astype(BF16)
        logits = jnp.dot(normed, tile_weight, preferred_element_type=F32)
        gate[pl.ds(pl.multiple_of(step * 256, 256), 256), :] = sigmoid(logits)
        return carry

    lax.fori_loop(0, NI // 16, tile_gate, 0)

    for g, dy in enumerate(ROUND):
        y_from = lax.rem(row + 4 - dy, 4)
        received(g, lb.at[y_from, :, :, mate_low], rf.at[g])
        forward(8 + g, y_from, mate_low, (row, core_mate, depth))
    mate_other = lax.rem(other_low + 2, 4)
    for g, dy in enumerate(ROUND):
        y_from = lax.rem(row + 4 - dy, 4)
        received(4 + g, lb.at[y_from, :, :, other_low], rf.at[4 + g])
        received(8 + g, lb.at[y_from, :, :, mate_other], rf.at[8 + g])

    osc[:, (BASE + NJ) * HB : (BASE + NJ + 1) * HB, :] = jnp.zeros((4, HB, 128), F32)
    out_sends = []
    count = 0
    mine = x * 4 + row
    for stage, dx in enumerate(ROUND):
        x_from = lax.rem(x + 4 - dx, 4)
        for dy in ROUND:
            if (dx, dy) != (0, 0):
                y_from = lax.rem(row + 4 - dy, 4)
                n = NEAR.index((dx, dy))
                received(n, rb.at[x_from, y_from], rr.at[n])
        for h in range(HB):
            first = h * NJ // 16 * 16
            skew = h * NJ - first
            lhs = jnp.concatenate([rb[x_from, y, first : first + 64, :] for y in range(4)], axis=1)
            for half in range(2):
                rhs = jnp.concatenate(
                    [lb[half * 2 + q, h].reshape(512, NI) for q in range(2)], axis=1
                )
                sums = jnp.dot(lhs, rhs, preferred_element_type=F32)
                for q in range(2):
                    osc[half * 2 + q, pl.ds((BASE - skew) * HB + h, 64, stride=HB), :] = sums[
                        :, q * NI : (q + 1) * NI
                    ]
        for dz in (2, 1, 3, 0):
            to_depth = lax.rem(depth + dz, 4)
            for dy in ROUND:
                to_row = lax.rem(row + dy, 4)
                start = pl.multiple_of(BASE * HB + to_depth * (NT * HB), HB)
                block = osc[to_row, pl.ds(start, MSG), :].astype(BF16)
                target = cb.at[depth, mine]
                if (dx, dy, dz) == (0, 0, 0):
                    cb[depth, mine] = block
                    continue
                os_[stage, to_row, to_depth] = block
                copy = pltpu.make_async_remote_copy(
                    src_ref=os_.at[stage, to_row, to_depth], dst_ref=target,
                    send_sem=so.at[count], recv_sem=ro.at[count],
                    device_id=(to_row, x_from * 4 + low, to_depth), device_id_type=MESH,
                )
                copy.start()
                out_sends.append((dx, dy, dz, count, copy))
                count += 1

    for dx, dy, dz, n, copy in out_sends:
        x_at = lax.rem(x + dx, 4)
        y_at = lax.rem(row + 4 - dy, 4)
        d_at = lax.rem(depth + 4 - dz, 4)
        received(n, cb.at[d_at, x_at * 4 + y_at], ro.at[n])

    hg = jnp.broadcast_to(hgain[...], (128, 128)).T
    hb = jnp.broadcast_to(hbias[...], (128, 128)).T
    weight = wo[...]

    def finish(j, sums):
        centre = jnp.mean(sums, axis=0, keepdims=True)
        shifted = sums - centre
        spread = jnp.mean(shifted * shifted, axis=0, keepdims=True)
        hidden = (shifted * lax.rsqrt(spread + EPSILON) * hg + hb).astype(BF16)
        projected = lax.dot_general(
            hidden, weight, (((0,), (0,)), ((), ())), preferred_element_type=F32
        )
        fin[pl.ds(j, NI, stride=16), :] = projected

    def pair_of_columns(p, carry):
        rows = pl.ds(pl.multiple_of(p * 16, 16), 16)
        total = cb[0, :, rows, :].astype(F32)
        for z in range(1, 4):
            total = total + cb[z, :, rows, :].astype(F32)
        finish(p * 2, total[:, :HB].reshape(128, NI))
        finish(p * 2 + 1, total[:, HB:].reshape(128, NI))
        return carry

    lax.fori_loop(0, JPAD // 2, pair_of_columns, 0)

    def write(step, carry):
        rows = pl.ds(pl.multiple_of(step * 256, 256), 256)
        result = (gate[rows, :] * fin[rows, :]).reshape(16, 16, 128)
        out[pl.ds(step * 16, 16)] = result[:, :NT, :].astype(BF16)
        return carry

    lax.fori_loop(0, NI // 16, write, 0)

    for copy in list(left_sends.values()) + list(right_sends.values()) + forwards:
        copy.wait_send()
    for item in out_sends:
        item[4].wait_send()


def per_device(
    left_pair, right_pair, pair_tile, row_flags, column_flags, key_flags,
    input_gain, input_bias, left_gate_weight, left_value_weight,
    right_gate_weight, right_value_weight, hidden_gain, hidden_bias,
    output_gate_weight, output_weight,
):
    vmem = pl.BlockSpec(memory_space=pltpu.VMEM)
    smem = pl.BlockSpec(memory_space=pltpu.SMEM)
    dma = pltpu.SemaphoreType.DMA
    return pl.pallas_call(
        kernel,
        out_shape=jax.ShapeDtypeStruct((NI, NT, 128), BF16),
        in_specs=[vmem] * 4 + [smem] * 2 + [vmem] * 11,
        out_specs=vmem,
        scratch_shapes=[
            pltpu.VMEM((NI * NM, 128), F32),
            pltpu.VMEM((16 * HB * NM, 128), F32),
            pltpu.VMEM((16 * HB * NJ, 128), F32),
            pltpu.VMEM((16, HB, NM, NI), BF16),
            pltpu.VMEM((4, HB, 4, 4, NM, NI), BF16),
            pltpu.VMEM((16, HB * NJ, NK), BF16),
            pltpu.VMEM((4, 4, HB * NJ, NK), BF16),
            pltpu.VMEM((4, SLOTS * HB, 128), F32),
            pltpu.VMEM((4, 4, 4, MSG, 128), BF16),
            pltpu.VMEM((4, 16, MSG, 128), BF16),
            pltpu.VMEM((NI * 16, 128), F32),
            pltpu.VMEM((NI * 16, 128), F32),
            dma((16,)), dma((16,)), dma((16,)), dma((16,)),
            dma((12,)), dma((12,)), dma((63,)), dma((63,)), dma((1,)),
        ],
        compiler_params=pltpu.CompilerParams(
            collective_id=0, has_side_effects=True, vmem_limit_bytes=48 * 2**20
        ),
        name="triangle",
    )(
        left_pair.reshape(NI * NM, 128),
        right_pair.reshape(NJ * NK, 128),
        pair_tile,
        row_flags.reshape(1, NI),
        column_flags,
        key_flags,
        key_flags,
        input_gain.reshape(1, 128),
        input_bias.reshape(1, 128),
        left_gate_weight, left_value_weight, right_gate_weight, right_value_weight,
        hidden_gain.reshape(1, 128),
        hidden_bias.reshape(1, 128),
        output_gate_weight, output_weight,
    )


def solution(mesh):
    in_specs = (
        P("row", "depth", "col", None),
        P("col", "depth", "row", None),
        P("row", ("col", "depth"), None),
        P("row"),
        P("col"),
    ) + (P(),) * 11
    return jax.shard_map(
        per_device,
        mesh=mesh,
        in_specs=in_specs,
        out_specs=P("row", ("col", "depth"), None),
        check_vma=False,
    )
```

time: 318 us -> 114 us (0.36)
  waiting for transfers between devices: 237 us -> 0 us
  Pallas kernels: 0 us -> 99.1 us
  matrix products: 25.3 us -> 0 us
  other arithmetic: 21.7 us -> 0 us
  between operations: 13.3 us -> 0.03 us
  local copies, waits for them, and re-layouts: 20.2 us -> 14 us
    all_gather x2 -> x0, waiting for transfers between devices: 167 us -> none  [the longest x1 98.1 us: per_device(): lax.all_gather(left_act, 'col', axis=2, tiled=True)]
    pallas_call x0 -> x1, Pallas kernels: none -> 99.1 us  [per_device(): pl.pallas_call(kernel, out_shape=jax.ShapeDtypeStruct((NI, NT, 128), BF16...]
    reduce_scatter x1 -> x0, waiting for transfers between devices: 69.9 us -> none  [per_device(): owned = lax.psum_scatter(combined, 'depth', scatter_dimension=1, tiled=True)]
    dot_general x7 -> x0, matrix products: 25.3 us -> none  [the longest x1 13 us: per_device(): jnp.einsum('iqmh,jqmh->ijh', lax.all_gather(left_act, 'col', axis=2, tile...]
    dot_general x4 -> x0, local copies, waits for them, and re-layouts: 13.4 us -> none  [the longest x2 6.72 us: gated_values(): content = jnp.dot(normed, value_weight, preferred_element_type=jnp.float32)]
    unnamed x30 -> x31, local copies, waits for them, and re-layouts: 2.16 us -> 13.1 us
    convert_element_type x4 -> x0, other arithmetic: 9.98 us -> none  [the longest x2 9.2 us: gated_values(): return (mask[..., None] * gating * content).astype(jnp.bfloat16)]
    reduce_sum x8 -> x0, other arithmetic: 9.95 us -> none  [the longest x4 5.61 us: layer_norm(): spread = jnp.mean(shifted * shifted, axis=-1, keepdims=True)]
  transfers between devices with their start and end apart: 3 -> 0, of which waited for: 3 -> 0; matrix products, arithmetic and copies ran while one was open for 5% -> 0% of each run, Pallas kernels for 0% -> 0%
where the time goes in v1:
time: 114 us; the launch traced here: 113 us
  Pallas kernels  99.1 us (87%)
  local copies, waits for them, and re-layouts  14 us (12%)
    pallas_call x1, Pallas kernels, per_device(): pl.pallas_call(kernel, out_shape=jax.ShapeDtypeStruct((NI, NT, 128), BF16...  99.1 us
    unnamed x31, local copies, waits for them, and re-layouts  13.1 us

profile of v1, /device:TPU:1, one launch (start us, length us, event | category | flops | bytes accessed | tf_op | source)
XLA Modules:
  0.0 113.1 jit_solution(2602769430229905931)
XLA Ops:
  0.0 1.3 %copy.17.xt = bf16[128,13,128]{2,1,0:T(8,128)(2,1)S(1)} copy(bf16[128,13,128]{2,0,1:T(8,128)(2,1)} %param.18) | data formatting | bytes 851968 | tf_op args[2]
  1.3 0.0 copy-start
  1.3 1.4 %copy-done = bf16[52,1,128,128]{3,2,1,0:T(8,128)(2,1)S(1)} copy-done((bf16[52,1,128,128]{3,2,1,0:T(8,128)(2,1)S(1)}, bf16[52,1,128,128]{3,2,1,0:T(8,128)(2,1)}, u32[]{:S(2)}) %copy-start) | copy-done | bytes 1703960
  2.8 0.0 copy-start.1
  2.8 1.2 %copy-done.1 = bf16[128,1,32,128]{3,2,1,0:T(8,128)(2,1)S(1)} copy-done((bf16[128,1,32,128]{3,2,1,0:T(8,128)(2,1)S(1)}, bf16[128,1,32,128]{3,2,1,0:T(8,128)(2,1)}, u32[]{:S(2)}) %copy-start.1) | copy-done | bytes 1048600
  4.0 0.0 copy-start.2
  4.0 0.8 copy-done.2
  4.7 0.0 copy-start.3
  4.7 0.8 copy-done.3
  5.5 0.0 copy-start.4
  5.5 0.8 copy-done.4
  6.3 0.0 copy-start.5
  6.3 0.8 copy-done.5
  7.0 0.0 copy-start.6
  7.0 0.8 copy-done.6
  7.8 0.0 copy-start.7
  7.8 0.8 copy-done.7
  8.5 0.0 copy-start.8
  8.5 0.7 copy-done.8
  9.2 0.0 copy-start.9
  9.2 0.7 copy-done.9
  9.9 0.7 copy-done.10
  10.5 0.0 copy-start.11
  10.5 0.7 copy-done.11
  11.2 0.0 copy-start.12
  11.2 0.7 copy-done.12
  11.9 0.0 copy-start.13
  11.9 0.7 copy-done.13
  12.5 0.0 copy-start.14
  12.5 0.7 copy-done.14
  13.2 99.1 %triangle.1 = bf16[128,13,128]{2,1,0:T(8,128)(2,1)S(1)} custom-call(bf16[4096,128]{1,0:T(8,128)(2,1)S(1)} %bitcast.8, bf16[6656,128]{1,0:T(8,128)(2,1)S(1)} %bitcast.7, bf16[128,13,128]{2,1,0:T(8,128)(2,1)S(1)} %copy.17.xt, s32[1,128]{1,0:T(1,128)S(1)} %bitcast.9, s32[52]{0:T(128)S(1)} %copy-done.10, s32[4,512]{1,0:T(4,128)S(1)} %copy-done.8, ...), custom_call_target="tpu_custom_call" | custom-call | tf_op jit(solution)/shard_map/triangle/pallas_call | solution.py:305
  112.2 0.9 copy.18
  (1 shorter events, 0.0 us)
Async XLA Ops:
  1.3 1.5 %copy-start = (bf16[52,1,128,128]{3,2,1,0:T(8,128)(2,1)S(1)}, bf16[52,1,128,128]{3,2,1,0:T(8,128)(2,1)}, u32[]{:S(2)}) copy-start(bf16[52,1,128,128]{3,2,1,0:T(8,128)(2,1)} %param.17) | copy-start | bytes 5111812
  2.8 1.2 %copy-start.1 = (bf16[128,1,32,128]{3,2,1,0:T(8,128)(2,1)S(1)}, bf16[128,1,32,128]{3,2,1,0:T(8,128)(2,1)}, u32[]{:S(2)}) copy-start(bf16[128,1,32,128]{3,2,1,0:T(8,128)(2,1)} %param.16) | copy-start | bytes 3145732
  4.0 0.8 copy-start.2
  4.7 0.8 copy-start.3
  5.5 0.8 copy-start.4
  6.3 0.8 copy-start.5
  7.0 0.8 copy-start.6
  7.8 0.8 copy-start.7
  8.5 0.7 copy-start.8
  9.2 0.7 copy-start.9
  9.9 0.7 copy-start.10
  10.5 0.7 copy-start.11
  11.2 0.7 copy-start.12
  11.9 0.7 copy-start.13
  12.5 0.7 copy-start.14

commit v2 on v1

--- a/solution.py
+++ b/solution.py
@@ -20,7 +20,11 @@
 BASE = 16
 
 ROUND = (2, 1, 3, 0)
+VIA = ((2, 0), (1, 3))
 NEAR = [(dx, dy) for dx in ROUND for dy in ROUND]
+
+
+LOAD_ORDER = (0, 7, 8, 9, 10, 3, 5, 1, 11, 12, 4, 6, 2, 15, 13, 14, 16)
 
 
 def normalise(values):
@@ -38,13 +42,29 @@
     return lax.dot_general(left, right, (((1,), (1,)), ((), ())), preferred_element_type=F32)
 
 
-def kernel(
-    xl, xr, xt, row_flags, column_flags, key_scalars, key_rows,
-    gain, bias, wlg, wlv, wrg, wrv, hgain, hbias, wog, wo,
-    out,
-    nl, tl, tr, ls, lb, rs, rb, osc, os_, cb, gate, fin,
-    sl, rl, sr, rr, sf, rf, so, ro, cs,
-):
+def kernel(*refs):
+    sources, refs = refs[:17], refs[17:]
+    out, refs = refs[0], refs[1:]
+    held, refs = refs[:17], refs[17:]
+    (
+        xl, xr, xt, row_flags, column_flags, key_scalars, key_rows,
+        gain, bias, wlg, wlv, wrg, wrv, hgain, hbias, wog, wo,
+    ) = held
+    (
+        nl, tl, tr, ls, lb, rs, rb, osc, av, ar, os_, cb, gate,
+        sl, rl, sr, rr, sf, rf, sa, ra, so, ro, cs, loads,
+    ) = refs
+    pending = [
+        pltpu.make_async_copy(src, dst, loads.at[n])
+        for n, (src, dst) in enumerate(zip(sources, held))
+    ]
+    for n in LOAD_ORDER:
+        pending[n].start()
+
+    def loaded(*numbers):
+        for n in numbers:
+            pending[n].wait()
+
     row = lax.axis_index("row")
     col = lax.axis_index("col")
     depth = lax.axis_index("depth")
@@ -63,11 +83,12 @@
         )
 
     barrier = pltpu.get_barrier_semaphore()
-    peers = [at(dx, dy, dz) for dz in range(4) for dx, dy in NEAR if (dx, dy, dz) != (0, 0, 0)]
+    peers = [at(dx, dy, dz) for dz in (0, 1, 3) for dx, dy in NEAR if (dx, dy, dz) != (0, 0, 0)]
     peers += [(row, core_mate, depth), (row, z_mate, depth)]
     for peer in peers:
         pl.semaphore_signal(barrier, inc=1, device_id=peer, device_id_type=MESH)
 
+    loaded(0, 7, 8, 9, 10, 3, 5)
     gains, biases = gain[...], bias[...]
 
     def left_norm(step, carry):
@@ -115,6 +136,7 @@
         copy.start()
         left_sends[dx, dy] = copy
 
+    loaded(1, 11, 12, 4, 6)
     w_right = jnp.concatenate([wrg[...], wrv[...]], axis=1).astype(F32).T.astype(BF16)
     key_block = key_rows[:, pl.ds(pl.multiple_of(row * NK, NK), NK)].astype(F32)
     here = lax.broadcasted_iota(jnp.int32, (4, NK), 0) == depth
@@ -180,19 +202,15 @@
         forward(g, y_from, low, (row, z_mate, depth))
         forward(4 + g, y_from, low, (row, core_mate, depth))
 
+    loaded(2, 15, 13, 14, 16)
     tile_weight = wog[...]
 
-    def tile_gate(step, carry):
-        rows = pl.ds(step * 16, 16)
-        padded = jnp.concatenate(
-            [xt[rows].astype(F32), jnp.zeros((16, 16 - NT, 128), F32)], axis=1
-        ).reshape(256, 128)
-        normed = (normalise(padded) * gains + biases).astype(BF16)
-        logits = jnp.dot(normed, tile_weight, preferred_element_type=F32)
-        gate[pl.ds(pl.multiple_of(step * 256, 256), 256), :] = sigmoid(logits)
+    def tile_gate(j, carry):
+        normed = (normalise(xt[j].astype(F32)) * gains + biases).astype(BF16)
+        gate[j] = sigmoid(jnp.dot(normed, tile_weight, preferred_element_type=F32))
         return carry
 
-    lax.fori_loop(0, NI // 16, tile_gate, 0)
+    lax.fori_loop(0, NT, tile_gate, 0)
 
     for g, dy in enumerate(ROUND):
         y_from = lax.rem(row + 4 - dy, 4)
@@ -204,11 +222,15 @@
         received(4 + g, lb.at[y_from, :, :, other_low], rf.at[4 + g])
         received(8 + g, lb.at[y_from, :, :, mate_other], rf.at[8 + g])
 
-    osc[:, (BASE + NJ) * HB : (BASE + NJ + 1) * HB, :] = jnp.zeros((4, HB, 128), F32)
-    out_sends = []
-    count = 0
+    osc[:, :, (BASE + NJ) * HB : (BASE + NJ + 1) * HB, :] = jnp.zeros((4, 4, HB, 128), F32)
+    relays, out_sends = [], []
     mine = x * 4 + row
-    for stage, dx in enumerate(ROUND):
+
+    def block_of(stage, dy, dz):
+        start = pl.multiple_of(BASE * HB + lax.rem(depth + dz, 4) * (NT * HB), HB)
+        return osc[stage, lax.rem(row + dy, 4), pl.ds(start, MSG), :]
+
+    def contract(stage, dx):
         x_from = lax.rem(x + 4 - dx, 4)
         for dy in ROUND:
             if (dx, dy) != (0, 0):
@@ -225,34 +247,53 @@
                 )
                 sums = jnp.dot(lhs, rhs, preferred_element_type=F32)
                 for q in range(2):
-                    osc[half * 2 + q, pl.ds((BASE - skew) * HB + h, 64, stride=HB), :] = sums[
+                    osc[stage, half * 2 + q, pl.ds((BASE - skew) * HB + h, 64, stride=HB), :] = sums[
                         :, q * NI : (q + 1) * NI
                     ]
-        for dz in (2, 1, 3, 0):
-            to_depth = lax.rem(depth + dz, 4)
+        for side, dz in enumerate((1, 3)):
+            for k, dy in enumerate(VIA[side]):
+                av[stage, side, k] = block_of(stage, dy, 2).astype(BF16)
+            copy = pltpu.make_async_remote_copy(
+                src_ref=av.at[stage, side], dst_ref=ar.at[stage, side],
+                send_sem=sa.at[stage * 2 + side], recv_sem=ra.at[stage * 2 + side],
+                device_id=at(0, 0, dz), device_id_type=MESH,
+            )
+            copy.start()
+            relays.append(copy)
+
+    def distribute(stage, dx):
+        x_from = lax.rem(x + 4 - dx, 4)
+        for side in range(2):
+            received(stage * 2 + side, ar.at[stage, side], ra.at[stage * 2 + side])
+        for slot, dz in enumerate((1, 3, 0)):
             for dy in ROUND:
-                to_row = lax.rem(row + dy, 4)
-                start = pl.multiple_of(BASE * HB + to_depth * (NT * HB), HB)
-                block = osc[to_row, pl.ds(start, MSG), :].astype(BF16)
-                target = cb.at[depth, mine]
+                block = block_of(stage, dy, dz)
+                if slot < 2 and dy in VIA[slot]:
+                    block = block + ar[stage, slot, VIA[slot].index(dy)].astype(F32)
                 if (dx, dy, dz) == (0, 0, 0):
-                    cb[depth, mine] = block
+                    cb[slot, mine] = block.astype(BF16)
                     continue
-                os_[stage, to_row, to_depth] = block
+                to_row, to_depth = lax.rem(row + dy, 4), lax.rem(depth + dz, 4)
+                os_[stage, to_row, slot] = block.astype(BF16)
+                n = len(out_sends)
                 copy = pltpu.make_async_remote_copy(
-                    src_ref=os_.at[stage, to_row, to_depth], dst_ref=target,
-                    send_sem=so.at[count], recv_sem=ro.at[count],
+                    src_ref=os_.at[stage, to_row, slot], dst_ref=cb.at[slot, mine],
+                    send_sem=so.at[n], recv_sem=ro.at[n],
                     device_id=(to_row, x_from * 4 + low, to_depth), device_id_type=MESH,
                 )
                 copy.start()
-                out_sends.append((dx, dy, dz, count, copy))
-                count += 1
-
-    for dx, dy, dz, n, copy in out_sends:
+                out_sends.append((dx, dy, slot, n, copy))
+
+    for stage, dx in enumerate(ROUND):
+        contract(stage, dx)
+        if stage:
+            distribute(stage - 1, ROUND[stage - 1])
+    distribute(3, ROUND[3])
+
+    for dx, dy, slot, n, copy in out_sends:
         x_at = lax.rem(x + dx, 4)
         y_at = lax.rem(row + 4 - dy, 4)
-        d_at = lax.rem(depth + 4 - dz, 4)
-        received(n, cb.at[d_at, x_at * 4 + y_at], ro.at[n])
+        received(n, cb.at[slot, x_at * 4 + y_at], ro.at[n])
 
     hg = jnp.broadcast_to(hgain[...], (128, 128)).T
     hb = jnp.broadcast_to(hbias[...], (128, 128)).T
@@ -266,28 +307,24 @@
         projected = lax.dot_general(
             hidden, weight, (((0,), (0,)), ((), ())), preferred_element_type=F32
         )
-        fin[pl.ds(j, NI, stride=16), :] = projected
+        out[j] = (gate[j] * projected).astype(BF16)
 
     def pair_of_columns(p, carry):
         rows = pl.ds(pl.multiple_of(p * 16, 16), 16)
         total = cb[0, :, rows, :].astype(F32)
-        for z in range(1, 4):
+        for z in range(1, 3):
             total = total + cb[z, :, rows, :].astype(F32)
         finish(p * 2, total[:, :HB].reshape(128, NI))
-        finish(p * 2 + 1, total[:, HB:].reshape(128, NI))
+
+        @pl.when(p < JPAD // 2 - 1)
+        def _():
+            finish(p * 2 + 1, total[:, HB:].reshape(128, NI))
+
         return carry
 
     lax.fori_loop(0, JPAD // 2, pair_of_columns, 0)
 
-    def write(step, carry):
-        rows = pl.ds(pl.multiple_of(step * 256, 256), 256)
-        result = (gate[rows, :] * fin[rows, :]).reshape(16, 16, 128)
-        out[pl.ds(step * 16, 16)] = result[:, :NT, :].astype(BF16)
-        return carry
-
-    lax.fori_loop(0, NI // 16, write, 0)
-
-    for copy in list(left_sends.values()) + list(right_sends.values()) + forwards:
+    for copy in list(left_sends.values()) + list(right_sends.values()) + forwards + relays:
         copy.wait_send()
     for item in out_sends:
         item[4].wait_send()
@@ -299,38 +336,11 @@
     right_gate_weight, right_value_weight, hidden_gain, hidden_bias,
     output_gate_weight, output_weight,
 ):
-    vmem = pl.BlockSpec(memory_space=pltpu.VMEM)
-    smem = pl.BlockSpec(memory_space=pltpu.SMEM)
     dma = pltpu.SemaphoreType.DMA
-    return pl.pallas_call(
-        kernel,
-        out_shape=jax.ShapeDtypeStruct((NI, NT, 128), BF16),
-        in_specs=[vmem] * 4 + [smem] * 2 + [vmem] * 11,
-        out_specs=vmem,
-        scratch_shapes=[
-            pltpu.VMEM((NI * NM, 128), F32),
-            pltpu.VMEM((16 * HB * NM, 128), F32),
-            pltpu.VMEM((16 * HB * NJ, 128), F32),
-            pltpu.VMEM((16, HB, NM, NI), BF16),
-            pltpu.VMEM((4, HB, 4, 4, NM, NI), BF16),
-            pltpu.VMEM((16, HB * NJ, NK), BF16),
-            pltpu.VMEM((4, 4, HB * NJ, NK), BF16),
-            pltpu.VMEM((4, SLOTS * HB, 128), F32),
-            pltpu.VMEM((4, 4, 4, MSG, 128), BF16),
-            pltpu.VMEM((4, 16, MSG, 128), BF16),
-            pltpu.VMEM((NI * 16, 128), F32),
-            pltpu.VMEM((NI * 16, 128), F32),
-            dma((16,)), dma((16,)), dma((16,)), dma((16,)),
-            dma((12,)), dma((12,)), dma((63,)), dma((63,)), dma((1,)),
-        ],
-        compiler_params=pltpu.CompilerParams(
-            collective_id=0, has_side_effects=True, vmem_limit_bytes=48 * 2**20
-        ),
-        name="triangle",
-    )(
+    operands = (
         left_pair.reshape(NI * NM, 128),
         right_pair.reshape(NJ * NK, 128),
-        pair_tile,
+        pair_tile.transpose(1, 0, 2),
         row_flags.reshape(1, NI),
         column_flags,
         key_flags,
@@ -342,6 +352,39 @@
         hidden_bias.reshape(1, 128),
         output_gate_weight, output_weight,
     )
+    held = [
+        pltpu.SMEM(a.shape, a.dtype) if n in (4, 5) else pltpu.VMEM(a.shape, a.dtype)
+        for n, a in enumerate(operands)
+    ]
+    result = pl.pallas_call(
+        kernel,
+        out_shape=jax.ShapeDtypeStruct((NT, NI, 128), BF16),
+        in_specs=[pl.BlockSpec(memory_space=pltpu.HBM)] * len(operands),
+        out_specs=pl.BlockSpec(memory_space=pltpu.VMEM),
+        scratch_shapes=held + [
+            pltpu.VMEM((NI * NM, 128), F32),
+            pltpu.VMEM((16 * HB * NM, 128), F32),
+            pltpu.VMEM((16 * HB * NJ, 128), F32),
+            pltpu.VMEM((16, HB, NM, NI), BF16),
+            pltpu.VMEM((4, HB, 4, 4, NM, NI), BF16),
+            pltpu.VMEM((16, HB * NJ, NK), BF16),
+            pltpu.VMEM((4, 4, HB * NJ, NK), BF16),
+            pltpu.VMEM((4, 4, SLOTS * HB, 128), F32),
+            pltpu.VMEM((4, 2, 2, MSG, 128), BF16),
+            pltpu.VMEM((4, 2, 2, MSG, 128), BF16),
+            pltpu.VMEM((4, 4, 3, MSG, 128), BF16),
+            pltpu.VMEM((3, 16, MSG, 128), BF16),
+            pltpu.VMEM((NT, NI, 128), F32),
+            dma((16,)), dma((16,)), dma((16,)), dma((16,)),
+            dma((12,)), dma((12,)), dma((8,)), dma((8,)),
+            dma((47,)), dma((47,)), dma((1,)), dma((17,)),
+        ],
+        compiler_params=pltpu.CompilerParams(
+            collective_id=0, has_side_effects=True, vmem_limit_bytes=60 * 2**20
+        ),
+        name="triangle",
+    )(*operands)
+    return result.transpose(1, 0, 2)
 
 
 def solution(mesh):

time: 114 us -> 93.6 us (0.82)
  local copies, waits for them, and re-layouts: 14 us -> 1.8 us
  Pallas kernels: 99.1 us -> 90.8 us
    unnamed x31 -> x1, local copies, waits for them, and re-layouts: 13.1 us -> 1.8 us
    pallas_call x1, Pallas kernels: 99.1 us -> 90.8 us  [per_device(): pl.pallas_call(kernel, out_shape=jax.ShapeDtypeStruct((NT, NI, 128), BF16...]
where the time goes in v2:
time: 93.6 us; the launch traced here: 92.6 us
  Pallas kernels  90.8 us (97%)
  local copies, waits for them, and re-layouts  1.8 us (2%)
    pallas_call x1, Pallas kernels, per_device(): pl.pallas_call(kernel, out_shape=jax.ShapeDtypeStruct((NT, NI, 128), BF16...  90.8 us

profile of v2, /device:TPU:1, one launch (start us, length us, event | category | flops | bytes accessed | tf_op | source)
XLA Modules:
  0.0 92.6 jit_solution(17222048882471911102)
XLA Ops:
  0.0 90.8 %triangle.1 = bf16[13,128,128]{2,1,0:T(8,128)(2,1)} custom-call(bf16[4096,128]{1,0:T(8,128)(2,1)} %bitcast.11, bf16[6656,128]{1,0:T(8,128)(2,1)} %bitcast.9, bf16[13,128,128]{2,1,0:T(8,128)(2,1)} %bitcast.12, s32[1,128]{1,0:T(1,128)} %bitcast.13, s32[52]{0:T(128)} %refs_4_.1, s32[4,512]{1,0:T(4,128)} %refs_6_.1, s32[4,512]{1,0:T(4,128)} %refs_6_.1, ...), custom_call_target="tpu_custom_call" | custom-call | tf_op jit(solution)/shard_map/triangle/pallas_call | solution.py:359
  90.8 1.8 %copy.18 = bf16[128,13,128]{2,0,1:T(8,128)(2,1)} copy(bf16[128,13,128]{2,0,1:T(8,128)(2,1)} %bitcast.10) | data formatting | bytes 851968

commit v3 on v2

--- a/solution.py
+++ b/solution.py
@@ -21,13 +21,20 @@
 
 ROUND = (2, 1, 3, 0)
 VIA = ((2, 0), (1, 3))
-NEAR = [(dx, dy) for dx in ROUND for dy in ROUND]
+def hops(offset):
+    return sum(min(d, 4 - d) for d in offset)
+
+
+STAGED = [(dx, dy) for dx in ROUND for dy in ROUND]
+NEAR = sorted([(dx, dy) for dx in ROUND for dy in ROUND], key=hops, reverse=True)
+DIRECT = [offset for offset in NEAR if hops(offset) <= 0]
 
 
 LOAD_ORDER = (0, 7, 8, 9, 10, 3, 5, 1, 11, 12, 4, 6, 2, 15, 13, 14, 16)
 
 
 def normalise(values):
+    values = values.astype(F32)
     centre = jnp.mean(values, axis=-1, keepdims=True)
     shifted = values - centre
     spread = jnp.mean(shifted * shifted, axis=-1, keepdims=True)
@@ -52,7 +59,7 @@
     ) = held
     (
         nl, tl, tr, ls, lb, rs, rb, osc, av, ar, os_, cb, gate,
-        sl, rl, sr, rr, sf, rf, sa, ra, so, ro, cs, loads,
+        sl, rl, sr, rr, sz, rz, sc, rc, sa, ra, so, ro, cs, loads,
     ) = refs
     pending = [
         pltpu.make_async_copy(src, dst, loads.at[n])
@@ -84,7 +91,10 @@
 
     barrier = pltpu.get_barrier_semaphore()
     peers = [at(dx, dy, dz) for dz in (0, 1, 3) for dx, dy in NEAR if (dx, dy, dz) != (0, 0, 0)]
-    peers += [(row, core_mate, depth), (row, z_mate, depth)]
+    peers.append((row, core_mate, depth))
+    for offset in DIRECT:
+        to_row, to_col, _ = at(*offset)
+        peers.append((to_row, to_col - low + mate_low, depth))
     for peer in peers:
         pl.semaphore_signal(barrier, inc=1, device_id=peer, device_id_type=MESH)
 
@@ -92,35 +102,53 @@
     gains, biases = gain[...], bias[...]
 
     def left_norm(step, carry):
-        rows = pl.ds(pl.multiple_of(step * 256, 256), 256)
-        nl[rows, :] = normalise(xl[rows, :].astype(F32)) * gains + biases
+        rows = pl.ds(pl.multiple_of(step * 512, 512), 512)
+        nl[rows, :] = normalise(xl[rows, :]) * gains + biases
         return carry
 
-    lax.fori_loop(0, NI * NM // 256, left_norm, 0)
+    lax.fori_loop(0, NI * NM // 512, left_norm, 0)
     w_left = jnp.concatenate([wlg[...], wlv[...]], axis=1).astype(F32).T.astype(BF16)
     row_mask = row_flags[...].astype(F32)
 
     def left_act(step, carry):
         xs = jnp.concatenate(
-            [nl[pl.ds(step * 4 + mm, NI, stride=NM), :] for mm in range(4)], axis=0
+            [nl[pl.ds(step * 8 + mm, NI, stride=NM), :] for mm in range(8)], axis=0
         ).astype(BF16)
         both = dot_nt(w_left, xs)
         act = sigmoid(both[:128]) * both[128:]
-        for mm in range(4):
-            key = key_scalars[depth, col * NM + step * 4 + mm].astype(F32)
+        for mm in range(8):
+            key = key_scalars[depth, col * NM + step * 8 + mm].astype(F32)
             part = act[:, mm * NI : (mm + 1) * NI] * (row_mask * key)
             for d in range(16):
-                tl[pl.ds(d * HB * NM + step * 4 + mm, HB, stride=NM), :] = part[d * HB : (d + 1) * HB]
+                tl[pl.ds(d * HB * NM + step * 8 + mm, HB, stride=NM), :] = part[d * HB : (d + 1) * HB]
         return carry
 
-    lax.fori_loop(0, NM // 4, left_act, 0)
+    lax.fori_loop(0, NM // 8, left_act, 0)
 
     pl.semaphore_wait(barrier, len(peers))
 
     def owner(dx, dy):
         return lax.rem(x + dx, 4) * 4 + lax.rem(row + dy, 4)
 
-    left_sends = {}
+    sends = []
+
+    def send(src, dst, send_sem, recv_sem, device):
+        copy = pltpu.make_async_remote_copy(
+            src_ref=src, dst_ref=dst, send_sem=send_sem, recv_sem=recv_sem,
+            device_id=device, device_id_type=MESH,
+        )
+        copy.start()
+        sends.append(copy)
+
+    def received(dst, sem):
+        pltpu.make_async_remote_copy(
+            src_ref=dst, dst_ref=dst, send_sem=sem, recv_sem=sem,
+            device_id=at(1, 0), device_id_type=MESH,
+        ).wait_recv()
+
+    def source(dx, dy):
+        return lax.rem(x + 4 - dx, 4), lax.rem(row + 4 - dy, 4)
+
     for n, (dx, dy) in enumerate(NEAR):
         d = owner(dx, dy)
         rows = pl.ds(pl.multiple_of(d * HB * NM, HB * NM), HB * NM)
@@ -128,13 +156,12 @@
         target = lb.at[row, :, x, low]
         if (dx, dy) == (0, 0):
             pltpu.make_async_copy(ls.at[d], target, cs.at[0]).start()
-            continue
-        copy = pltpu.make_async_remote_copy(
-            src_ref=ls.at[d], dst_ref=target, send_sem=sl.at[n], recv_sem=rl.at[n],
-            device_id=at(dx, dy), device_id_type=MESH,
-        )
-        copy.start()
-        left_sends[dx, dy] = copy
+            send(ls.at[d], target, sc.at[n], rc.at[n], (row, core_mate, depth))
+        else:
+            send(ls.at[d], target, sl.at[n], rl.at[n], at(dx, dy))
+        if (dx, dy) in DIRECT:
+            to_row, to_col, _ = at(dx, dy)
+            send(ls.at[d], target, sz.at[n], rz.at[n], (to_row, to_col - low + mate_low, depth))
 
     loaded(1, 11, 12, 4, 6)
     w_right = jnp.concatenate([wrg[...], wrv[...]], axis=1).astype(F32).T.astype(BF16)
@@ -143,87 +170,62 @@
     key_mask = jnp.sum(jnp.where(here, key_block, 0.0), axis=0, keepdims=True)
 
     def right_act(step, carry):
-        rows = pl.ds(pl.multiple_of(step * 512, 512), 512)
-        xs = (normalise(xr[rows, :].astype(F32)) * gains + biases).astype(BF16)
+        rows = pl.ds(pl.multiple_of(step * 1664, 128), 1664)
+        xs = (normalise(xr[rows, :]) * gains + biases).astype(BF16)
         both = dot_nt(w_right, xs)
         act = sigmoid(both[:128]) * both[128:]
-        for jj in range(4):
-            flag = column_flags[step * 4 + jj].astype(F32)
+        for jj in range(13):
+            flag = column_flags[step * 13 + jj].astype(F32)
             part = act[:, jj * NK : (jj + 1) * NK] * (key_mask * flag)
             for d in range(16):
-                tr[pl.ds(d * HB * NJ + step * 4 + jj, HB, stride=NJ), :] = part[d * HB : (d + 1) * HB]
+                tr[pl.ds(d * HB * NJ + step * 13 + jj, HB, stride=NJ), :] = part[d * HB : (d + 1) * HB]
         return carry
 
-    lax.fori_loop(0, NJ // 4, right_act, 0)
-
-    right_sends = {}
-    for n, (dx, dy) in enumerate(NEAR):
+    lax.fori_loop(0, NJ // 13, right_act, 0)
+
+    for n, (dx, dy) in enumerate(STAGED):
         d = owner(dx, dy)
         rows = pl.ds(pl.multiple_of(d * HB * NJ, HB * NJ), HB * NJ)
         if (dx, dy) == (0, 0):
             rb[x, row] = tr[rows, :].astype(BF16)
             continue
         rs[d] = tr[rows, :].astype(BF16)
-        copy = pltpu.make_async_remote_copy(
-            src_ref=rs.at[d], dst_ref=rb.at[x, row], send_sem=sr.at[n], recv_sem=rr.at[n],
-            device_id=at(dx, dy), device_id_type=MESH,
-        )
-        copy.start()
-        right_sends[dx, dy] = copy
-
-    def received(n, dst, sem):
-        pltpu.make_async_remote_copy(
-            src_ref=dst, dst_ref=dst, send_sem=sem, recv_sem=sem,
-            device_id=at(1, 0), device_id_type=MESH,
-        ).wait_recv()
-
-    def source(dx, dy):
-        return lax.rem(x + 4 - dx, 4), lax.rem(row + 4 - dy, 4)
-
-    forwards = []
-
-    def forward(n, y_from, share, device):
-        part = lb.at[y_from, :, :, share]
-        copy = pltpu.make_async_remote_copy(
-            src_ref=part, dst_ref=part, send_sem=sf.at[n], recv_sem=rf.at[n],
-            device_id=device, device_id_type=MESH,
-        )
-        copy.start()
-        forwards.append(copy)
+        send(rs.at[d], rb.at[x, row], sr.at[n], rr.at[n], at(dx, dy))
 
     pltpu.make_async_copy(ls.at[owner(0, 0)], lb.at[row, :, x, low], cs.at[0]).wait()
-    for g, dy in enumerate(ROUND):
-        for dx in ROUND:
-            if (dx, dy) != (0, 0):
-                x_from, y_from = source(dx, dy)
-                n = NEAR.index((dx, dy))
-                received(n, lb.at[y_from, :, x_from, low], rl.at[n])
-        y_from = lax.rem(row + 4 - dy, 4)
-        forward(g, y_from, low, (row, z_mate, depth))
-        forward(4 + g, y_from, low, (row, core_mate, depth))
+    for n, offset in enumerate(NEAR):
+        if offset == (0, 0):
+            continue
+        x_from, y_from = source(*offset)
+        part = lb.at[y_from, :, x_from, low]
+        received(part, rl.at[n])
+        if offset not in DIRECT:
+            send(part, part, sz.at[n], rz.at[n], (row, z_mate, depth))
+        send(part, part, sc.at[n], rc.at[n], (row, core_mate, depth))
 
     loaded(2, 15, 13, 14, 16)
     tile_weight = wog[...]
 
     def tile_gate(j, carry):
-        normed = (normalise(xt[j].astype(F32)) * gains + biases).astype(BF16)
+        normed = (normalise(xt[j]) * gains + biases).astype(BF16)
         gate[j] = sigmoid(jnp.dot(normed, tile_weight, preferred_element_type=F32))
         return carry
 
     lax.fori_loop(0, NT, tile_gate, 0)
 
-    for g, dy in enumerate(ROUND):
-        y_from = lax.rem(row + 4 - dy, 4)
-        received(g, lb.at[y_from, :, :, mate_low], rf.at[g])
-        forward(8 + g, y_from, mate_low, (row, core_mate, depth))
+    for n, offset in reversed(list(enumerate(NEAR))):
+        x_from, y_from = source(*offset)
+        part = lb.at[y_from, :, x_from, mate_low]
+        received(part, rz.at[n])
+        send(part, part, sc.at[16 + n], rc.at[16 + n], (row, core_mate, depth))
     mate_other = lax.rem(other_low + 2, 4)
-    for g, dy in enumerate(ROUND):
-        y_from = lax.rem(row + 4 - dy, 4)
-        received(4 + g, lb.at[y_from, :, :, other_low], rf.at[4 + g])
-        received(8 + g, lb.at[y_from, :, :, mate_other], rf.at[8 + g])
+    for n, offset in enumerate(NEAR):
+        x_from, y_from = source(*offset)
+        received(lb.at[y_from, :, x_from, other_low], rc.at[n])
+        received(lb.at[y_from, :, x_from, mate_other], rc.at[16 + n])
 
     osc[:, :, (BASE + NJ) * HB : (BASE + NJ + 1) * HB, :] = jnp.zeros((4, 4, HB, 128), F32)
-    relays, out_sends = [], []
+    out_sends = []
     mine = x * 4 + row
 
     def block_of(stage, dy, dz):
@@ -235,8 +237,7 @@
         for dy in ROUND:
             if (dx, dy) != (0, 0):
                 y_from = lax.rem(row + 4 - dy, 4)
-                n = NEAR.index((dx, dy))
-                received(n, rb.at[x_from, y_from], rr.at[n])
+                received(rb.at[x_from, y_from], rr.at[STAGED.index((dx, dy))])
         for h in range(HB):
             first = h * NJ // 16 * 16
             skew = h * NJ - first
@@ -253,18 +254,13 @@
         for side, dz in enumerate((1, 3)):
             for k, dy in enumerate(VIA[side]):
                 av[stage, side, k] = block_of(stage, dy, 2).astype(BF16)
-            copy = pltpu.make_async_remote_copy(
-                src_ref=av.at[stage, side], dst_ref=ar.at[stage, side],
-                send_sem=sa.at[stage * 2 + side], recv_sem=ra.at[stage * 2 + side],
-                device_id=at(0, 0, dz), device_id_type=MESH,
-            )
-            copy.start()
-            relays.append(copy)
+            sems = sa.at[stage * 2 + side], ra.at[stage * 2 + side]
+            send(av.at[stage, side], ar.at[stage, side], *sems, at(0, 0, dz))
 
     def distribute(stage, dx):
         x_from = lax.rem(x + 4 - dx, 4)
         for side in range(2):
-            received(stage * 2 + side, ar.at[stage, side], ra.at[stage * 2 + side])
+            received(ar.at[stage, side], ra.at[stage * 2 + side])
         for slot, dz in enumerate((1, 3, 0)):
             for dy in ROUND:
                 block = block_of(stage, dy, dz)
@@ -276,13 +272,9 @@
                 to_row, to_depth = lax.rem(row + dy, 4), lax.rem(depth + dz, 4)
                 os_[stage, to_row, slot] = block.astype(BF16)
                 n = len(out_sends)
-                copy = pltpu.make_async_remote_copy(
-                    src_ref=os_.at[stage, to_row, slot], dst_ref=cb.at[slot, mine],
-                    send_sem=so.at[n], recv_sem=ro.at[n],
-                    device_id=(to_row, x_from * 4 + low, to_depth), device_id_type=MESH,
-                )
-                copy.start()
-                out_sends.append((dx, dy, slot, n, copy))
+                target = (to_row, x_from * 4 + low, to_depth)
+                send(os_.at[stage, to_row, slot], cb.at[slot, mine], so.at[n], ro.at[n], target)
+                out_sends.append((dx, dy, slot))
 
     for stage, dx in enumerate(ROUND):
         contract(stage, dx)
@@ -290,10 +282,10 @@
             distribute(stage - 1, ROUND[stage - 1])
     distribute(3, ROUND[3])
 
-    for dx, dy, slot, n, copy in out_sends:
+    for n, (dx, dy, slot) in enumerate(out_sends):
         x_at = lax.rem(x + dx, 4)
         y_at = lax.rem(row + 4 - dy, 4)
-        received(n, cb.at[slot, x_at * 4 + y_at], ro.at[n])
+        received(cb.at[slot, x_at * 4 + y_at], ro.at[n])
 
     hg = jnp.broadcast_to(hgain[...], (128, 128)).T
     hb = jnp.broadcast_to(hbias[...], (128, 128)).T
@@ -309,25 +301,17 @@
         )
         out[j] = (gate[j] * projected).astype(BF16)
 
-    def pair_of_columns(p, carry):
-        rows = pl.ds(pl.multiple_of(p * 16, 16), 16)
+    for p in range(JPAD // 2):
+        rows = slice(p * 16, p * 16 + 16)
         total = cb[0, :, rows, :].astype(F32)
         for z in range(1, 3):
             total = total + cb[z, :, rows, :].astype(F32)
         finish(p * 2, total[:, :HB].reshape(128, NI))
-
-        @pl.when(p < JPAD // 2 - 1)
-        def _():
+        if p < JPAD // 2 - 1:
             finish(p * 2 + 1, total[:, HB:].reshape(128, NI))
 
-        return carry
-
-    lax.fori_loop(0, JPAD // 2, pair_of_columns, 0)
-
-    for copy in list(left_sends.values()) + list(right_sends.values()) + forwards + relays:
+    for copy in sends:
         copy.wait_send()
-    for item in out_sends:
-        item[4].wait_send()
 
 
 def per_device(
@@ -376,7 +360,7 @@
             pltpu.VMEM((3, 16, MSG, 128), BF16),
             pltpu.VMEM((NT, NI, 128), F32),
             dma((16,)), dma((16,)), dma((16,)), dma((16,)),
-            dma((12,)), dma((12,)), dma((8,)), dma((8,)),
+            dma((16,)), dma((16,)), dma((32,)), dma((32,)), dma((8,)), dma((8,)),
             dma((47,)), dma((47,)), dma((1,)), dma((17,)),
         ],
         compiler_params=pltpu.CompilerParams(

time: 93.6 us -> 83.9 us (0.90)
  Pallas kernels: 90.8 us -> 82 us
    pallas_call x1, Pallas kernels: 90.8 us -> 82 us  [per_device(): pl.pallas_call(kernel, out_shape=jax.ShapeDtypeStruct((NT, NI, 128), BF16...]
where the time goes in v3:
time: 83.9 us; the launch traced here: 83.8 us
  Pallas kernels  82 us (98%)
  local copies, waits for them, and re-layouts  1.8 us (2%)
    pallas_call x1, Pallas kernels, per_device(): pl.pallas_call(kernel, out_shape=jax.ShapeDtypeStruct((NT, NI, 128), BF16...  82 us
    unnamed x1, local copies, waits for them, and re-layouts  1.8 us

profile of v3, /device:TPU:1, one launch (start us, length us, event | category | flops | bytes accessed | tf_op | source)
XLA Modules:
  0.0 83.8 jit_solution(11978392904682947003)
XLA Ops:
  0.0 82.0 %triangle.1 = bf16[13,128,128]{2,1,0:T(8,128)(2,1)} custom-call(bf16[4096,128]{1,0:T(8,128)(2,1)} %bitcast.11, bf16[6656,128]{1,0:T(8,128)(2,1)} %bitcast.9, bf16[13,128,128]{2,1,0:T(8,128)(2,1)} %bitcast.12, s32[1,128]{1,0:T(1,128)} %bitcast.13, s32[52]{0:T(128)} %refs_4_.1, s32[4,512]{1,0:T(4,128)} %refs_6_.1, s32[4,512]{1,0:T(4,128)} %refs_6_.1, ...), custom_call_target="tpu_custom_call" | custom-call | tf_op jit(solution)/shard_map/triangle/pallas_call | solution.py:343
  82.0 1.8 %copy.18 = bf16[128,13,128]{2,0,1:T(8,128)(2,1)} copy(bf16[128,13,128]{2,0,1:T(8,128)(2,1)} %bitcast.10) | data formatting | bytes 851968

commit v4 on v3

--- a/solution.py
+++ b/solution.py
@@ -18,6 +18,8 @@
 MSG = JPAD * HB
 SLOTS = 80
 BASE = 16
+
+LEFT, ACROSS, CORE, CORE_ACROSS, RIGHT, RELAY, OUT = range(7)
 
 ROUND = (2, 1, 3, 0)
 VIA = ((2, 0), (1, 3))
@@ -59,7 +61,7 @@
     ) = held
     (
         nl, tl, tr, ls, lb, rs, rb, osc, av, ar, os_, cb, gate,
-        sl, rl, sr, rr, sz, rz, sc, rc, sa, ra, so, ro, cs, loads,
+        sent, rl, rr, rz, rc, ra, ro, cs, loads,
     ) = refs
     pending = [
         pltpu.make_async_copy(src, dst, loads.at[n])
@@ -130,15 +132,11 @@
     def owner(dx, dy):
         return lax.rem(x + dx, 4) * 4 + lax.rem(row + dy, 4)
 
-    sends = []
-
-    def send(src, dst, send_sem, recv_sem, device):
-        copy = pltpu.make_async_remote_copy(
-            src_ref=src, dst_ref=dst, send_sem=send_sem, recv_sem=recv_sem,
+    def send(src, dst, kind, recv_sem, device):
+        pltpu.make_async_remote_copy(
+            src_ref=src, dst_ref=dst, send_sem=sent.at[kind], recv_sem=recv_sem,
             device_id=device, device_id_type=MESH,
-        )
-        copy.start()
-        sends.append(copy)
+        ).start()
 
     def received(dst, sem):
         pltpu.make_async_remote_copy(
@@ -156,12 +154,12 @@
         target = lb.at[row, :, x, low]
         if (dx, dy) == (0, 0):
             pltpu.make_async_copy(ls.at[d], target, cs.at[0]).start()
-            send(ls.at[d], target, sc.at[n], rc.at[n], (row, core_mate, depth))
+            send(ls.at[d], target, CORE, rc.at[0], (row, core_mate, depth))
         else:
-            send(ls.at[d], target, sl.at[n], rl.at[n], at(dx, dy))
+            send(ls.at[d], target, LEFT, rl.at[n], at(dx, dy))
         if (dx, dy) in DIRECT:
             to_row, to_col, _ = at(dx, dy)
-            send(ls.at[d], target, sz.at[n], rz.at[n], (to_row, to_col - low + mate_low, depth))
+            send(ls.at[d], target, ACROSS, rz.at[n], (to_row, to_col - low + mate_low, depth))
 
     loaded(1, 11, 12, 4, 6)
     w_right = jnp.concatenate([wrg[...], wrv[...]], axis=1).astype(F32).T.astype(BF16)
@@ -190,7 +188,7 @@
             rb[x, row] = tr[rows, :].astype(BF16)
             continue
         rs[d] = tr[rows, :].astype(BF16)
-        send(rs.at[d], rb.at[x, row], sr.at[n], rr.at[n], at(dx, dy))
+        send(rs.at[d], rb.at[x, row], RIGHT, rr.at[ROUND.index(dx)], at(dx, dy))
 
     pltpu.make_async_copy(ls.at[owner(0, 0)], lb.at[row, :, x, low], cs.at[0]).wait()
     for n, offset in enumerate(NEAR):
@@ -200,29 +198,17 @@
         part = lb.at[y_from, :, x_from, low]
         received(part, rl.at[n])
         if offset not in DIRECT:
-            send(part, part, sz.at[n], rz.at[n], (row, z_mate, depth))
-        send(part, part, sc.at[n], rc.at[n], (row, core_mate, depth))
-
-    loaded(2, 15, 13, 14, 16)
-    tile_weight = wog[...]
-
-    def tile_gate(j, carry):
-        normed = (normalise(xt[j]) * gains + biases).astype(BF16)
-        gate[j] = sigmoid(jnp.dot(normed, tile_weight, preferred_element_type=F32))
-        return carry
-
-    lax.fori_loop(0, NT, tile_gate, 0)
+            send(part, part, ACROSS, rz.at[n], (row, z_mate, depth))
+        send(part, part, CORE, rc.at[0], (row, core_mate, depth))
 
     for n, offset in reversed(list(enumerate(NEAR))):
         x_from, y_from = source(*offset)
         part = lb.at[y_from, :, x_from, mate_low]
         received(part, rz.at[n])
-        send(part, part, sc.at[16 + n], rc.at[16 + n], (row, core_mate, depth))
+        send(part, part, CORE_ACROSS, rc.at[1], (row, core_mate, depth))
     mate_other = lax.rem(other_low + 2, 4)
-    for n, offset in enumerate(NEAR):
-        x_from, y_from = source(*offset)
-        received(lb.at[y_from, :, x_from, other_low], rc.at[n])
-        received(lb.at[y_from, :, x_from, mate_other], rc.at[16 + n])
+    received(lb.at[:, :, :, other_low], rc.at[0])
+    received(lb.at[:, :, :, mate_other], rc.at[1])
 
     osc[:, :, (BASE + NJ) * HB : (BASE + NJ + 1) * HB, :] = jnp.zeros((4, 4, HB, 128), F32)
     out_sends = []
@@ -234,10 +220,7 @@
 
     def contract(stage, dx):
         x_from = lax.rem(x + 4 - dx, 4)
-        for dy in ROUND:
-            if (dx, dy) != (0, 0):
-                y_from = lax.rem(row + 4 - dy, 4)
-                received(rb.at[x_from, y_from], rr.at[STAGED.index((dx, dy))])
+        received(rb.at[x_from] if dx else rb.at[x_from, pl.ds(0, 3)], rr.at[stage])
         for h in range(HB):
             first = h * NJ // 16 * 16
             skew = h * NJ - first
@@ -254,38 +237,42 @@
         for side, dz in enumerate((1, 3)):
             for k, dy in enumerate(VIA[side]):
                 av[stage, side, k] = block_of(stage, dy, 2).astype(BF16)
-            sems = sa.at[stage * 2 + side], ra.at[stage * 2 + side]
-            send(av.at[stage, side], ar.at[stage, side], *sems, at(0, 0, dz))
+            send(av.at[stage, side], ar.at[stage, side], RELAY, ra.at[stage], at(0, 0, dz))
 
     def distribute(stage, dx):
         x_from = lax.rem(x + 4 - dx, 4)
-        for side in range(2):
-            received(ar.at[stage, side], ra.at[stage * 2 + side])
+        received(ar.at[stage], ra.at[stage])
         for slot, dz in enumerate((1, 3, 0)):
             for dy in ROUND:
                 block = block_of(stage, dy, dz)
                 if slot < 2 and dy in VIA[slot]:
                     block = block + ar[stage, slot, VIA[slot].index(dy)].astype(F32)
                 if (dx, dy, dz) == (0, 0, 0):
-                    cb[slot, mine] = block.astype(BF16)
+                    cb[slot * 16 + mine] = block.astype(BF16)
                     continue
                 to_row, to_depth = lax.rem(row + dy, 4), lax.rem(depth + dz, 4)
-                os_[stage, to_row, slot] = block.astype(BF16)
                 n = len(out_sends)
+                os_[n] = block.astype(BF16)
                 target = (to_row, x_from * 4 + low, to_depth)
-                send(os_.at[stage, to_row, slot], cb.at[slot, mine], so.at[n], ro.at[n], target)
+                send(os_.at[n], cb.at[slot * 16 + mine], OUT, ro.at[0], target)
                 out_sends.append((dx, dy, slot))
 
     for stage, dx in enumerate(ROUND):
         contract(stage, dx)
-        if stage:
-            distribute(stage - 1, ROUND[stage - 1])
-    distribute(3, ROUND[3])
-
-    for n, (dx, dy, slot) in enumerate(out_sends):
-        x_at = lax.rem(x + dx, 4)
-        y_at = lax.rem(row + 4 - dy, 4)
-        received(cb.at[slot, x_at * 4 + y_at], ro.at[n])
+    for stage, dx in enumerate(ROUND):
+        distribute(stage, dx)
+
+    loaded(2, 15, 13, 14, 16)
+    tile_weight = wog[...]
+
+    def tile_gate(j, carry):
+        normed = (normalise(xt[j]) * gains + biases).astype(BF16)
+        gate[j] = sigmoid(jnp.dot(normed, tile_weight, preferred_element_type=F32))
+        return carry
+
+    lax.fori_loop(0, NT, tile_gate, 0)
+
+    received(cb.at[pl.ds(0, 47)], ro.at[0])
 
     hg = jnp.broadcast_to(hgain[...], (128, 128)).T
     hb = jnp.broadcast_to(hbias[...], (128, 128)).T
@@ -303,15 +290,21 @@
 
     for p in range(JPAD // 2):
         rows = slice(p * 16, p * 16 + 16)
-        total = cb[0, :, rows, :].astype(F32)
+        total = cb[0:16, rows, :].astype(F32)
         for z in range(1, 3):
-            total = total + cb[z, :, rows, :].astype(F32)
+            total = total + cb[z * 16 : z * 16 + 16, rows, :].astype(F32)
         finish(p * 2, total[:, :HB].reshape(128, NI))
         if p < JPAD // 2 - 1:
             finish(p * 2 + 1, total[:, HB:].reshape(128, NI))
 
-    for copy in sends:
-        copy.wait_send()
+    for kind, part in (
+        (LEFT, ls.at[pl.ds(0, 15)]), (ACROSS, ls), (CORE, ls), (CORE_ACROSS, ls),
+        (RIGHT, rs.at[pl.ds(0, 15)]), (RELAY, av), (OUT, os_),
+    ):
+        pltpu.make_async_remote_copy(
+            src_ref=part, dst_ref=part, send_sem=sent.at[kind], recv_sem=sent.at[kind],
+            device_id=at(1, 0), device_id_type=MESH,
+        ).wait_send()
 
 
 def per_device(
@@ -356,12 +349,11 @@
             pltpu.VMEM((4, 4, SLOTS * HB, 128), F32),
             pltpu.VMEM((4, 2, 2, MSG, 128), BF16),
             pltpu.VMEM((4, 2, 2, MSG, 128), BF16),
-            pltpu.VMEM((4, 4, 3, MSG, 128), BF16),
-            pltpu.VMEM((3, 16, MSG, 128), BF16),
+            pltpu.VMEM((47, MSG, 128), BF16),
+            pltpu.VMEM((48, MSG, 128), BF16),
             pltpu.VMEM((NT, NI, 128), F32),
-            dma((16,)), dma((16,)), dma((16,)), dma((16,)),
-            dma((16,)), dma((16,)), dma((32,)), dma((32,)), dma((8,)), dma((8,)),
-            dma((47,)), dma((47,)), dma((1,)), dma((17,)),
+            dma((7,)), dma((15,)), dma((4,)), dma((16,)), dma((2,)), dma((4,)),
+            dma((1,)), dma((1,)), dma((17,)),
         ],
         compiler_params=pltpu.CompilerParams(
             collective_id=0, has_side_effects=True, vmem_limit_bytes=60 * 2**20

time: 83.9 us -> 81.2 us (0.968)
  the two profiles are of different devices: /device:TPU:1 before, /device:TPU:4 now
where the time goes in v4:
time: 81.2 us; the launch traced here: 81.1 us
  Pallas kernels  79.3 us (98%)
  local copies, waits for them, and re-layouts  1.8 us (2%)
    pallas_call x1, Pallas kernels, per_device(): pl.pallas_call(kernel, out_shape=jax.ShapeDtypeStruct((NT, NI, 128), BF16...  79.3 us
    unnamed x1, local copies, waits for them, and re-layouts  1.8 us

profile of v4, /device:TPU:4, one launch (start us, length us, event | category | flops | bytes accessed | tf_op | source)
XLA Modules:
  0.0 81.1 jit_solution(6173060005885475374)
XLA Ops:
  0.0 79.3 %triangle.1 = bf16[13,128,128]{2,1,0:T(8,128)(2,1)} custom-call(bf16[4096,128]{1,0:T(8,128)(2,1)} %bitcast.11, bf16[6656,128]{1,0:T(8,128)(2,1)} %bitcast.9, bf16[13,128,128]{2,1,0:T(8,128)(2,1)} %bitcast.12, s32[1,128]{1,0:T(1,128)} %bitcast.13, s32[52]{0:T(128)} %refs_4_.1, s32[4,512]{1,0:T(4,128)} %refs_6_.1, s32[4,512]{1,0:T(4,128)} %refs_6_.1, ...), custom_call_target="tpu_custom_call" | custom-call | tf_op jit(solution)/shard_map/triangle/pallas_call | solution.py:336
  79.3 1.8 %copy.18 = bf16[128,13,128]{2,0,1:T(8,128)(2,1)} copy(bf16[128,13,128]{2,0,1:T(8,128)(2,1)} %bitcast.10) | data formatting | bytes 851968

commit v5 on v4

--- a/solution.py
+++ b/solution.py
@@ -67,7 +67,18 @@
         pltpu.make_async_copy(src, dst, loads.at[n])
         for n, (src, dst) in enumerate(zip(sources, held))
     ]
-    for n in LOAD_ORDER:
+    half = NI * NM // 2
+    first_half, second_half = [
+        pltpu.make_async_copy(
+            sources[0].at[pl.ds(k * half, half)], xl.at[pl.ds(k * half, half)], loads.at[17 * k]
+        )
+        for k in range(2)
+    ]
+    first_half.start()
+    for n in LOAD_ORDER[1:3]:
+        pending[n].start()
+    second_half.start()
+    for n in LOAD_ORDER[3:]:
         pending[n].start()
 
     def loaded(*numbers):
@@ -100,15 +111,19 @@
     for peer in peers:
         pl.semaphore_signal(barrier, inc=1, device_id=peer, device_id_type=MESH)
 
-    loaded(0, 7, 8, 9, 10, 3, 5)
+    first_half.wait()
+    loaded(7, 8)
     gains, biases = gain[...], bias[...]
 
     def left_norm(step, carry):
-        rows = pl.ds(pl.multiple_of(step * 512, 512), 512)
+        rows = pl.ds(pl.multiple_of(step * 1024, 1024), 1024)
         nl[rows, :] = normalise(xl[rows, :]) * gains + biases
         return carry
 
-    lax.fori_loop(0, NI * NM // 512, left_norm, 0)
+    lax.fori_loop(0, NI * NM // 2048, left_norm, 0)
+    second_half.wait()
+    lax.fori_loop(NI * NM // 2048, NI * NM // 1024, left_norm, 0)
+    loaded(9, 10, 3, 5)
     w_left = jnp.concatenate([wlg[...], wlv[...]], axis=1).astype(F32).T.astype(BF16)
     row_mask = row_flags[...].astype(F32)
 
@@ -201,7 +216,7 @@
             send(part, part, ACROSS, rz.at[n], (row, z_mate, depth))
         send(part, part, CORE, rc.at[0], (row, core_mate, depth))
 
-    for n, offset in reversed(list(enumerate(NEAR))):
+    for n, offset in [(15, (0, 0))] + list(enumerate(NEAR))[:15]:
         x_from, y_from = source(*offset)
         part = lb.at[y_from, :, x_from, mate_low]
         received(part, rz.at[n])
@@ -259,8 +274,9 @@
 
     for stage, dx in enumerate(ROUND):
         contract(stage, dx)
-    for stage, dx in enumerate(ROUND):
-        distribute(stage, dx)
+        if stage:
+            distribute(stage - 1, ROUND[stage - 1])
+    distribute(3, ROUND[3])
 
     loaded(2, 15, 13, 14, 16)
     tile_weight = wog[...]
@@ -353,7 +369,7 @@
             pltpu.VMEM((48, MSG, 128), BF16),
             pltpu.VMEM((NT, NI, 128), F32),
             dma((7,)), dma((15,)), dma((4,)), dma((16,)), dma((2,)), dma((4,)),
-            dma((1,)), dma((1,)), dma((17,)),
+            dma((1,)), dma((1,)), dma((18,)),
         ],
         compiler_params=pltpu.CompilerParams(
             collective_id=0, has_side_effects=True, vmem_limit_bytes=60 * 2**20

time: 81.2 us -> 80.2 us (0.988)
  the two profiles are of different devices: /device:TPU:4 before, /device:TPU:1 now
where the time goes in v5:
time: 80.2 us; the launch traced here: 79.2 us
  Pallas kernels  77.4 us (97%)
  local copies, waits for them, and re-layouts  1.8 us (2%)
    pallas_call x1, Pallas kernels, per_device(): pl.pallas_call(kernel, out_shape=jax.ShapeDtypeStruct((NT, NI, 128), BF16...  77.4 us
    unnamed x1, local copies, waits for them, and re-layouts  1.8 us

profile of v5, /device:TPU:1, one launch (start us, length us, event | category | flops | bytes accessed | tf_op | source)
XLA Modules:
  0.0 79.2 jit_solution(6441294862917626685)
XLA Ops:
  0.0 77.4 %triangle.1 = bf16[13,128,128]{2,1,0:T(8,128)(2,1)} custom-call(bf16[4096,128]{1,0:T(8,128)(2,1)} %bitcast.11, bf16[6656,128]{1,0:T(8,128)(2,1)} %bitcast.9, bf16[13,128,128]{2,1,0:T(8,128)(2,1)} %bitcast.12, s32[1,128]{1,0:T(1,128)} %bitcast.13, s32[52]{0:T(128)} %refs_4_.1, s32[4,512]{1,0:T(4,128)} %refs_6_.1, s32[4,512]{1,0:T(4,128)} %refs_6_.1, ...), custom_call_target="tpu_custom_call" | custom-call | tf_op jit(solution)/shard_map/triangle/pallas_call | solution.py:352
  77.4 1.8 %copy.18 = bf16[128,13,128]{2,0,1:T(8,128)(2,1)} copy(bf16[128,13,128]{2,0,1:T(8,128)(2,1)} %bitcast.10) | data formatting | bytes 851968
